TPU v7x, 32 devices: a whole 2x2x4 slice. The times are simulated.
32 devices in a mesh: runs: 2 (over y), sec: 4 (over z), mpo: 2 (over x), rep: 2 (over core).
Axes of the slice: x: 2, y: 2, z: 4, core: 2. Of those that a mesh axis runs over, the one named last changes fastest.
Arguments:
- wavefunction: bfloat16 [128, 256, 256], P(('runs', 'sec'), None, 'rep'), parts along dimension 0, may hold values from -6 to 6
- left_env: bfloat16 [16, 10, 256, 256], P(('runs', 'sec'), 'mpo'), parts along dimension 0, may hold values from -0.375 to 0.375
- right_env: bfloat16 [16, 10, 256, 256], P(('runs', 'sec'), 'mpo', None, 'rep'), parts along dimension 0, may hold values from -0.125 to 0.125
- send_order: int32 [4, 16], P('sec'), may hold values from 0 to 15, each once within a row
- recv_order: int32 [4, 16], P('sec'), may hold values from 0 to 15, each once within a row
- pair_left: int32 [4, 16], P('sec'), may hold values from 0 to 1
- pair_right: int32 [4, 16], P('sec'), may hold values from 0 to 1
- left_size: int32 [8], P('sec'), may hold values from 128 to 256
- right_size: int32 [8], P('sec'), may hold values from 128 to 256
- mpo_pattern: int32 [8, 10], P('sec', 'mpo'), may hold values 0 or 1
Outputs:
- applied: bfloat16 [128, 256, 256], P(('runs', 'sec'), 'mpo', 'rep'), parts along dimension 0
There are 2 independent parts, one for each index of `runs`. A program takes and returns all parts, laid end to end along the dimension named above; an argument that names none is the same for every part. Nothing has to cross between parts.
Inputs may be any that keep to these rules, and one draw needn't show every extreme that they name: `send_order`: each row names each of 0 to 15 once. `recv_order`: each row names each of 0 to 15 once.
All inputs are finite; a program needn't handle non-finite values. No bound on the sum of `mpo_pattern` on one device may be relied on, other than what follows from the above.
Results may differ from a plain program's by a relative error of at most 0.0051.
Values may be sent and summed in bfloat16 or wider, within the bound.
A program may use at most 128 MiB of HBM per device.

v0:
```python
import jax
import jax.numpy as jnp
from jax import lax
from jax.sharding import PartitionSpec as P


def local(
    wavefunction,
    left_env,
    right_env,
    send_order,
    recv_order,
    pair_left,
    pair_right,
    left_size,
    right_size,
    mpo_pattern,
):
    pair_count = wavefunction.shape[0]
    block_width = wavefunction.shape[1]
    half_cols = wavefunction.shape[2]
    peer_count = lax.axis_size("sec")
    per_peer = pair_count // peer_count
    send_rows = send_order[0]
    row_index = jnp.arange(block_width, dtype=jnp.int32)
    left_ids = pair_left[0][send_rows]
    keep_left = (row_index[None, :] < left_size[left_ids][:, None]).astype(jnp.float32)
    weights = mpo_pattern[left_ids].astype(jnp.float32)
    source = lax.all_gather(wavefunction, "rep", axis=2, tiled=True)
    source = source[send_rows] * keep_left[:, :, None].astype(jnp.bfloat16)
    left_blocks = left_env[left_ids]
    interim = jnp.einsum("pwik,pkj->pwij", left_blocks, source, preferred_element_type=jnp.float32)
    interim = (interim * (keep_left[:, None, :, None] * weights[:, :, None, None])).astype(
        jnp.bfloat16
    )
    outgoing = interim.reshape((peer_count, per_peer) + interim.shape[1:])
    arrived = lax.all_to_all(outgoing, "sec", split_axis=0, concat_axis=0, tiled=True)
    arrived = arrived.reshape(interim.shape)[recv_order[0]]
    right_ids = pair_right[0]
    right_len = right_size[right_ids]
    rep_start = lax.axis_index("rep") * half_cols
    keep_rows = (row_index[None, :] < right_len[:, None]).astype(jnp.bfloat16)
    col_index = jnp.arange(half_cols, dtype=jnp.int32) + rep_start
    keep_cols = (col_index[None, :] < right_len[:, None]).astype(jnp.bfloat16)
    right_blocks = right_env[right_ids] * keep_rows[:, None, :, None] * keep_cols[:, None, None, :]
    partial_value = jnp.einsum(
        "pwik,pwkj->pij", arrived, right_blocks, preferred_element_type=jnp.float32
    )
    return lax.psum_scatter(partial_value, "mpo", scatter_dimension=1, tiled=True).astype(
        jnp.bfloat16
    )


def solution(mesh):
    placed = (
        P(("runs", "sec"), None, "rep"),
        P(("runs", "sec"), "mpo", None, None),
        P(("runs", "sec"), "mpo", None, "rep"),
        P("sec", None),
        P("sec", None),
        P("sec", None),
        P("sec", None),
        P("sec"),
        P("sec"),
        P("sec", "mpo"),
    )
    return jax.shard_map(
        local,
        mesh=mesh,
        in_specs=placed,
        out_specs=P(("runs", "sec"), "mpo", "rep"),
        check_vma=False,
    )
```

profile of v0, /device:TPU:0, one launch (start us, length us, event | category | flops | bytes accessed | tf_op | source)
XLA Modules:
  0.0 327.0 jit_solution(10866559425940692248)
XLA Ops:
  6.5 0.0 copy-start
  6.5 0.0 all-gather.2.cloned.1.call-start
  6.5 0.7 all-gather.2.cloned.1.call-update
  7.3 0.7 fusion.14
  7.9 1.3 gather_fusion
  9.3 1.2 gather_fusion.3
  10.5 0.0 copy-done
  10.5 0.0 copy-start.2
  10.5 5.7 %gather_fusion.1 = bf16[16,5,256,256]{3,2,1,0:T(8,128)(2,1)} fusion(bf16[2,5,256,256]{3,2,1,0:T(8,128)(2,1)S(1)} %copy-done, s32[1024]{0:T(1024)S(1)} %pad_clamp_fusion.2), kind=kCustom, calls=%fused_computation.1 | custom fusion | bytes 20971584 | tf_op jit(solution)/shard_map/gather | solution.py:31
  16.2 0.0 copy-done.2
  16.2 0.6 fusion.19
  16.9 1.3 compare_select_fusion.5
  18.1 0.1 fusion.13
  18.2 0.1 broadcast_multiply_fusion
  18.3 3.7 %all-gather.2.cloned.1.call-done = bf16[16,256,256]{2,1,0:T(8,128)(2,1)} async-done(((bf16[16,256,128]{2,1,0:T(8,128)(2,1)}), bf16[16,256,256]{2,1,0:T(8,128)(2,1)}) %all-gather.2.cloned.1.call-update) | async-done | bytes 2097168 | tf_op jit(solution)/shard_map/all_gather | solution.py:29
  21.9 2.3 gather_fusion.2
  24.2 8.2 %multiply_convert_fusion = bf16[16,5,256,256]{3,2,1,0:T(8,128)(2,1)} fusion(f32[16,5,256]{2,1,0:T(8,128)S(1)} %broadcast_multiply_fusion, bf16[16,5,256,256]{3,2,1,0:T(8,128)(2,1)} %gather_fusion.1, bf16[16,256,256]{2,1,0:T(8,128)(2,1)S(1)} %gather_fusion.2, bf16[16,256]{1,0:T(8,128)(2,1)S(1)} %get-tuple-element.7), kind=kOutput, calls=%fused_computation.6 | convolution fusion | flops 2695888896 | bytes 23158784 | tf_op jit(solution)/shard_map/pwik,pkj->pwij/dot_general | solution.py:32
  32.5 0.0 copy-start.4
  32.5 0.0 copy-start.1
  32.5 6.1 %all-to-all-start = ((bf16[4,4,5,256,256]{4,3,2,1,0:T(8,128)(2,1)}), bf16[4,4,5,256,256]{4,3,2,1,0:T(8,128)(2,1)}, u32[]{:S(2)}, u32[]{:S(2)}) async-start(bf16[4,4,5,256,256]{4,3,2,1,0:T(8,128)(2,1)} %bitcast.42), calls=%async_computation | async-start | bytes 20971520 | tf_op jit(solution)/shard_map/all_to_all | solution.py:37
  38.6 0.0 reduce-scatter.2.cloned.1.call-start
  38.6 0.0 copy-done.4
  38.7 0.0 copy-done.1
  38.7 0.0 copy-start.5
  38.7 0.0 copy-start.3
  38.7 3.6 %gather_fusion.5 = bf16[16,5,256,128]{3,2,1,0:T(8,128)(2,1)} fusion(bf16[2,5,256,128]{3,2,1,0:T(8,128)(2,1)S(1)} %copy-done.1, s32[1024]{0:T(1024)S(1)} %pad_clamp_fusion), kind=kCustom, calls=%fused_computation.5 | custom fusion | bytes 10485824 | tf_op jit(solution)/shard_map/gather | solution.py:45
  42.3 0.0 copy-done.5
  42.3 0.0 copy-done.3
  42.3 0.6 fusion.18
  42.9 1.3 compare_select_fusion.4
  44.2 0.1 compare_convert_fusion
  44.3 0.1 fusion.12
  44.4 223.0 %all-to-all-done = bf16[4,4,5,256,256]{4,3,2,1,0:T(8,128)(2,1)} async-done(((bf16[4,4,5,256,256]{4,3,2,1,0:T(8,128)(2,1)}), bf16[4,4,5,256,256]{4,3,2,1,0:T(8,128)(2,1)}, u32[]{:S(2)}, u32[]{:S(2)}) %all-to-all-start) | async-done | bytes 10485792 | tf_op jit(solution)/shard_map/all_to_all | solution.py:37
  267.4 9.6 %gather_fusion.4 = bf16[16,5,256,256]{3,2,1,0:T(8,128)(2,1)} fusion(bf16[16,5,256,256]{3,2,1,0:T(8,128)(2,1)} %bitcast.10, s32[1024]{0:T(1024)S(1)} %pad_clamp_fusion.1), kind=kCustom, calls=%fused_computation.4 | custom fusion | bytes 20971584 | tf_op jit(solution)/shard_map/gather | solution.py:38
  276.9 9.8 %fusion.7 = f32[16,256,128]{2,1,0:T(8,128)} fusion(bf16[16,5,256,256]{3,2,1,0:T(8,128)(2,1)} %gather_fusion.4, bf16[16,5,256,128]{3,2,1,0:T(8,128)(2,1)} %gather_fusion.5, bf16[16,128]{1,0:T(8,128)(2,1)S(1)} %compare_convert_fusion, bf16[16,256]{1,0:T(8,128)(2,1)S(1)} %fusion.12), kind=kOutput, calls=%fused_computation.14 | convolution fusion | flops 1347420160 | bytes 17838080 | tf_op jit(solution)/shard_map/pwik,pwkj->pij/dot_general | solution.py:46
  286.7 0.0 reduce-scatter.2.cloned.1.call-update
  286.7 31.3 %reduce-scatter.2.cloned.1.call-done = f32[16,128,128]{2,1,0:T(8,128)} async-done(((f32[16,256,128]{2,1,0:T(8,128)}), f32[16,128,128]{2,1,0:T(8,128)}) %reduce-scatter.2.cloned.1.call-update) | async-done | bytes 1048592 | tf_op jit(solution)/shard_map/reduce_scatter | solution.py:49
  318.1 2.1 convert_element_type.52
  (9 shorter events, 0.1 us)
Async XLA Ops:
  6.5 4.0 %copy-start = (bf16[2,5,256,256]{3,2,1,0:T(8,128)(2,1)S(1)}, bf16[2,5,256,256]{3,2,1,0:T(8,128)(2,1)}, u32[]{:S(2)}) copy-start(bf16[2,5,256,256]{3,2,1,0:T(8,128)(2,1)} %param.11) | copy-start | bytes 3932164
  6.5 15.4 %all-gather.2.cloned.1.call-start = ((), (), s32[]{:S(2)}) async-start(), calls=%async_computation.2 | async-start | bytes 3145728 | tf_op jit(solution)/shard_map/all_gather | solution.py:29
  10.5 5.7 %copy-start.2 = (s32[2]{0:T(128)S(1)}, s32[2]{0:T(128)}, u32[]{:S(2)}) copy-start(s32[2]{0:T(128)} %param.17) | copy-start | bytes 28
  32.5 6.2 %copy-start.4 = (s32[1,16]{1,0:T(1,128)S(1)}, s32[1,16]{1,0:T(1,128)}, u32[]{:S(2)}) copy-start(s32[1,16]{1,0:T(1,128)} %param.16) | copy-start | bytes 196
  32.5 6.2 %copy-start.1 = (bf16[2,5,256,128]{3,2,1,0:T(8,128)(2,1)S(1)}, bf16[2,5,256,128]{3,2,1,0:T(8,128)(2,1)}, u32[]{:S(2)}) copy-start(bf16[2,5,256,128]{3,2,1,0:T(8,128)(2,1)} %param.12) | copy-start | bytes 1966084
  32.5 234.9 %all-to-all-start = ((bf16[4,4,5,256,256]{4,3,2,1,0:T(8,128)(2,1)}), bf16[4,4,5,256,256]{4,3,2,1,0:T(8,128)(2,1)}, u32[]{:S(2)}, u32[]{:S(2)}) async-start(bf16[4,4,5,256,256]{4,3,2,1,0:T(8,128)(2,1)} %bitcast.42), calls=%async_computation | async-start | bytes 20971520 | tf_op jit(solution)/shard_map/all_to_all | solution.py:37
  38.6 279.5 %reduce-scatter.2.cloned.1.call-start = ((), (), s32[]{:S(2)}) async-start(), calls=%async_computation.3 | async-start | bytes 3145728 | tf_op jit(solution)/shard_map/reduce_scatter | solution.py:49
  38.7 3.6 %copy-start.5 = (s32[1,16]{1,0:T(1,128)S(1)}, s32[1,16]{1,0:T(1,128)}, u32[]{:S(2)}) copy-start(s32[1,16]{1,0:T(1,128)} %param.14) | copy-start | bytes 196
  38.7 3.6 %copy-start.3 = (s32[2]{0:T(128)S(1)}, s32[2]{0:T(128)}, u32[]{:S(2)}) copy-start(s32[2]{0:T(128)} %param.18) | copy-start | bytes 28
Sparse Core Ops, SparseCore 0:
  8.9 13.0 all-gather.1
  286.9 31.1 reduce-scatter.1
where the time goes:
time: 327 us
  waiting for transfers between devices  259 us (79%)
  local copies, waits for them, and re-layouts  24.9 us (8%)
  matrix products  18 us (6%)
  between operations  13.5 us (4%)
  starting transfers between devices  6.16 us (2%)
  other arithmetic  5.66 us (2%)
    all_to_all x1, waiting for transfers between devices, local(): lax.all_to_all(outgoing, 'sec', split_axis=0, concat_axis=0, tiled=True)  223 us
    reduce_scatter x1, waiting for transfers between devices, local(): lax.psum_scatter(partial_value, 'mpo', scatter_dimension=1, tiled=True)  31.3 us
    dot_general x1, matrix products, local(): jnp.einsum('pwik,pwkj->pij', arrived, right_blocks, preferred_element_typ...  9.77 us
    gather x1, local copies, waits for them, and re-layouts, local(): arrived = arrived.reshape(interim.shape)[recv_order[0]]  9.57 us
    dot_general x1, matrix products, local(): jnp.einsum('pwik,pkj->pwij', left_blocks, source, preferred_element_type=...  8.23 us
  transfers between devices with their start and end apart: 3, of which 3 were waited for; matrix products, arithmetic and copies ran while one was open for 5% of the time, Pallas kernels for 0%

commit v1 on v0

v1 whole, which is shorter than its diff:
```python
import jax
import jax.numpy as jnp
from jax import lax
from jax.sharding import PartitionSpec as P

BF = jnp.bfloat16
F32 = jnp.float32


def local(
    wavefunction,
    left_env,
    right_env,
    send_order,
    recv_order,
    pair_left,
    pair_right,
    left_size,
    right_size,
    mpo_pattern,
):
    width = wavefunction.shape[1]
    half = wavefunction.shape[2]
    pairs = wavefunction.shape[0]
    peers = lax.axis_size("sec")
    reps = lax.axis_size("rep")
    mpos = lax.axis_size("mpo")
    lefts, nw = left_env.shape[:2]
    send_rows = send_order[0]
    rows = jnp.arange(width, dtype=jnp.int32)
    left_ids = pair_left[0][send_rows]
    keep = (rows[None, :] < left_size[left_ids][:, None]).astype(BF)
    source = wavefunction[send_rows] * keep[:, :, None]
    tag = jnp.broadcast_to(left_ids.astype(BF)[:, None, None], (pairs, 16, half))
    source = jnp.concatenate([source, tag], axis=1)
    arrived = lax.all_to_all(source, "sec", split_axis=0, concat_axis=0, tiled=True)
    arrived = arrived[recv_order[0]]
    own = arrived[:, width, 0].astype(jnp.int32)
    left_of = own + (recv_order[0] // (pairs // peers)) * lefts
    arrived = lax.all_gather(arrived[:, :width], "rep", axis=2, tiled=True)

    keep_l = (rows[None, :] < left_size[:, None]).astype(BF)
    scale = keep_l[:, None, :, None] * mpo_pattern.astype(BF)[:, :, None, None]
    masked_left = left_env * scale
    part = width // reps
    mine = lax.dynamic_slice_in_dim(masked_left, lax.axis_index("rep") * part, part, axis=2)
    full = lax.all_gather(mine, "sec", axis=0, tiled=True)
    full = lax.all_gather(full, "rep", axis=2, tiled=True)
    blocks = full[left_of]
    interim = jnp.einsum("pwik,pkj->pwij", blocks, arrived, preferred_element_type=F32).astype(BF)

    right_ids = pair_right[0]
    keep_r = rows[None, :] < right_size[:, None]
    cols = jnp.arange(half, dtype=jnp.int32) + lax.axis_index("rep") * half
    keep_c = cols[None, :] < right_size[:, None]
    mask = (keep_r[:, :, None] & keep_c[:, None, :]).astype(BF)
    right_blocks = (right_env * mask[:, None])[right_ids]
    value = jnp.einsum("pwik,pwkj->pij", interim, right_blocks, preferred_element_type=F32)
    value = value.astype(BF).reshape(pairs, mpos, width // mpos, half)
    value = lax.all_to_all(value, "mpo", split_axis=1, concat_axis=1, tiled=True)
    return jnp.sum(value.astype(F32), axis=1).astype(BF)


def solution(mesh):
    placed = (
        P(("runs", "sec"), None, "rep"),
        P(("runs", "sec"), "mpo", None, None),
        P(("runs", "sec"), "mpo", None, "rep"),
        P("sec", None),
        P("sec", None),
        P("sec", None),
        P("sec", None),
        P("sec"),
        P("sec"),
        P("sec", "mpo"),
    )
    return jax.shard_map(
        local,
        mesh=mesh,
        in_specs=placed,
        out_specs=P(("runs", "sec"), "mpo", "rep"),
        check_vma=False,
    )
```

time: 327 us -> 154 us (0.47)
  waiting for transfers between devices: 259 us -> 84.9 us
  blocking collectives: 0 us -> 15.3 us
  local copies, waits for them, and re-layouts: 24.9 us -> 16.3 us
  matrix products: 18 us -> 11.8 us
    all_to_all x1, waiting for transfers between devices: 223 us -> 27.2 us  [local(): lax.all_to_all(source, 'sec', split_axis=0, concat_axis=0, tiled=True)]
    all_gather x1 -> x3, waiting for transfers between devices: 3.67 us -> 57.6 us  [the longest x1 57.6 us: local(): full = lax.all_gather(mine, 'sec', axis=0, tiled=True)]
    reduce_scatter x1 -> x0, waiting for transfers between devices: 31.3 us -> none  [local(): lax.psum_scatter(partial_value, 'mpo', scatter_dimension=1, tiled=True)]
    all_to_all x0 -> x1, blocking collectives: none -> 15.3 us  [local(): lax.all_to_all(value, 'mpo', split_axis=1, concat_axis=1, tiled=True)]
    gather x7 -> x5, local copies, waits for them, and re-layouts: 23.6 us -> 14.3 us  [the longest x1 8.71 us: local(): blocks = full[left_of]]
    dot_general x2 -> x1, matrix products: 18 us -> 11.8 us  [local(): jnp.einsum('pwik,pwkj->pij', interim, right_blocks, preferred_element_typ...]
  transfers between devices with their start and end apart: 3 -> 4, of which waited for: 3 -> 2; matrix products, arithmetic and copies ran while one was open for 5% -> 13% of each run, Pallas kernels for 0% -> 0%
where the time goes in v1:
time: 154 us
  waiting for transfers between devices  84.9 us (55%)
  local copies, waits for them, and re-layouts  16.3 us (11%)
  blocking collectives  15.3 us (10%)
  between operations  13.3 us (9%)
  matrix products  11.8 us (8%)
  other arithmetic  8.79 us (6%)
  starting transfers between devices  3.64 us (2%)
    all_gather x1, waiting for transfers between devices, local(): full = lax.all_gather(mine, 'sec', axis=0, tiled=True)  57.6 us
    all_to_all x1, waiting for transfers between devices, local(): lax.all_to_all(source, 'sec', split_axis=0, concat_axis=0, tiled=True)  27.2 us
    all_to_all x1, blocking collectives, local(): lax.all_to_all(value, 'mpo', split_axis=1, concat_axis=1, tiled=True)  15.3 us
    dot_general x1, matrix products, local(): jnp.einsum('pwik,pwkj->pij', interim, right_blocks, preferred_element_typ...  11.8 us
    gather x1, local copies, waits for them, and re-layouts, local(): blocks = full[left_of]  8.71 us
    all_to_all x1, starting transfers between devices, local(): lax.all_to_all(source, 'sec', split_axis=0, concat_axis=0, tiled=True)  3.56 us
    gather x1, local copies, waits for them, and re-layouts, local(): right_blocks = (right_env * mask[:, None])[right_ids]  3.48 us
  transfers between devices with their start and end apart: 4, of which 2 were waited for; matrix products, arithmetic and copies ran while one was open for 13% of the time, Pallas kernels for 0%

profile of v1, /device:TPU:0, one launch (start us, length us, event | category | flops | bytes accessed | tf_op | source)
XLA Modules:
  0.0 154.1 jit_solution(13632132100700562179)
XLA Ops:
  6.5 0.0 copy-start
  6.5 0.0 all-gather.4.cloned.1.call-start
  6.5 0.8 compare_convert_fusion
  7.4 0.7 convert_element_type.53
  8.0 0.1 broadcast_multiply_fusion.2
  8.1 0.0 copy-start.5
  8.1 2.2 %dynamic-slice_multiply_fusion = bf16[2,5,128,256]{3,2,1,0:T(8,128)(2,1)} fusion(bf16[2,5,256,256]{3,2,1,0:T(8,128)(2,1)} %param.11, s32[]{:T(128)S(6)} %select_n.66, bf16[2,5,128]{2,1,0:T(8,128)(2,1)S(1)} %constant_dynamic-slice_fusion), kind=kLoop, calls=%fused_computation.11 | loop fusion | flops 1310720 | bytes 1313284 | tf_op jit(solution)/shard_map/mul | solution.py:44
  10.3 0.0 all-gather.4.cloned.1.call-update
  10.3 0.0 all-gather.6.cloned.1.call-start
  10.4 57.6 %all-gather.4.cloned.1.call-done = bf16[8,5,128,256]{3,2,1,0:T(8,128)(2,1)} async-done(((bf16[2,5,128,256]{3,2,1,0:T(8,128)(2,1)}), bf16[8,5,128,256]{3,2,1,0:T(8,128)(2,1)}) %all-gather.4.cloned.1.call-update) | async-done | bytes 2621456 | tf_op jit(solution)/shard_map/all_gather | solution.py:47
  68.0 0.0 all-gather.6.cloned.1.call-update
  68.0 0.0 copy-done.5
  68.1 0.0 copy-done.1
  68.1 0.7 gather_fusion.1
  68.7 0.0 copy-done
  68.7 0.8 gather_fusion
  69.5 0.0 copy-done.3
  69.5 0.6 fusion.17
  70.1 0.0 copy-done.4
  70.1 1.3 fusion.13
  71.4 0.1 fusion.10
  71.5 0.7 broadcast_multiply_fusion
  72.2 0.1 broadcast_in_dim.2
  72.3 0.0 copy-start.7
  72.3 1.1 pad_maximum_fusion
  73.4 3.6 %all-to-all-start = ((bf16[16,272,128]{2,1,0:T(8,128)(2,1)}), bf16[16,272,128]{2,1,0:T(8,128)(2,1)S(1)}, u32[]{:S(2)}, u32[]{:S(2)}) async-start(bf16[16,272,128]{2,1,0:T(8,128)(2,1)} %pad_maximum_fusion), calls=%async_computation | async-start | bytes 2228224 | tf_op jit(solution)/shard_map/all_to_all | solution.py:36
  76.9 0.0 all-gather.8.cloned.1.call-start
  77.0 0.0 copy-done.7
  77.0 0.0 copy-start.6
  77.0 27.2 %all-to-all-done = bf16[16,272,128]{2,1,0:T(8,128)(2,1)S(1)} async-done(((bf16[16,272,128]{2,1,0:T(8,128)(2,1)}), bf16[16,272,128]{2,1,0:T(8,128)(2,1)S(1)}, u32[]{:S(2)}, u32[]{:S(2)}) %all-to-all-start) | async-done | bytes 1114144 | tf_op jit(solution)/shard_map/all_to_all | solution.py:36
  104.3 0.8 gather_fusion.2
  105.0 0.0 copy-start.2
  105.1 1.1 slice.22
  106.2 0.0 all-gather.8.cloned.1.call-update
  106.2 0.0 copy-done.6
  106.2 0.1 iota_compare_fusion.1
  106.3 0.1 broadcast_compare_fusion
  106.4 0.1 and_convert_fusion
  106.5 0.0 copy-done.2
  106.5 0.1 broadcast_multiply_fusion.1
  106.6 3.5 %gather_fusion.4 = bf16[16,5,256,128]{3,2,1,0:T(8,128)(2,1)} fusion(bf16[2,5,256,128]{3,2,1,0:T(8,128)(2,1)S(1)} %broadcast_multiply_fusion.1, s32[1024]{0:T(1024)S(1)} %pad_clamp_fusion), kind=kCustom, calls=%fused_computation.4 | custom fusion | bytes 10485824 | tf_op jit(solution)/shard_map/gather | solution.py:57
  110.1 0.4 fusion.11
  110.5 0.0 all-gather.6.cloned.1.call-done
  110.5 8.7 %gather_fusion.3 = bf16[16,5,256,256]{3,2,1,0:T(8,128)(2,1)} fusion(bf16[8,5,256,256]{3,2,1,0:T(8,128)(2,1)} %all-gather.6.cloned.1.call-done, s32[1024]{0:T(1024)S(1)} %pad_clamp_fusion.1), kind=kCustom, calls=%fused_computation.3 | custom fusion | bytes 20971584 | tf_op jit(solution)/shard_map/gather | solution.py:49
  119.2 11.8 %bitcast_convert_fusion = bf16[16,256,128]{2,1,0:T(8,128)(2,1)S(1)} fusion(bf16[16,5,256,128]{3,2,1,0:T(8,128)(2,1)} %gather_fusion.4, bf16[16,5,256,256]{3,2,1,0:T(8,128)(2,1)} %gather_fusion.3, bf16[16,256,256]{2,1,0:T(8,128)(2,1)} %all-gather.8.cloned.1.call-done), kind=kOutput, calls=%fused_computation.9 | convolution fusion | flops 4032299008 | bytes 18874368 | tf_op jit(solution)/shard_map/pwik,pwkj->pij/dot_general | solution.py:58
  131.0 0.1 copy.11
  131.1 15.3 %all_to_all.10 = bf16[16,2,128,128]{3,2,0,1:T(8,128)(2,1)S(1)} all-to-all(bf16[16,2,128,128]{3,2,0,1:T(8,128)(2,1)S(1)} %copy.11), channel_id=1, replica_groups=mesh['runs'=2,'sec'=4,'mpo'=2,'rep'=2] {'mpo'}, dimensions={1} | all-to-all | bytes 2097152 | tf_op jit(solution)/shard_map/all_to_all | solution.py:60
  146.4 1.1 reduce_sum.12
  (14 shorter events, 0.1 us)
Async XLA Ops:
  6.5 62.2 %copy-start = (bf16[16,256,128]{2,1,0:T(8,128)(2,1)S(1)}, bf16[16,256,128]{2,1,0:T(8,128)(2,1)}, u32[]{:S(2)}) copy-start(bf16[16,256,128]{2,1,0:T(8,128)(2,1)} %param.10) | copy-start | bytes 3145732
  6.5 61.5 %all-gather.4.cloned.1.call-start = ((), (), s32[]{:S(2)}) async-start(), calls=%async_computation.2 | async-start | bytes 3276800 | tf_op jit(solution)/shard_map/all_gather | solution.py:47
  8.1 59.9 %copy-start.5 = (s32[1,16]{1,0:T(1,128)S(1)}, s32[1,16]{1,0:T(1,128)}, u32[]{:S(2)}) copy-start(s32[1,16]{1,0:T(1,128)} %param.13) | copy-start | bytes 196
  8.1 60.0 %copy-start.1 = (s32[1,16]{1,0:T(1,128)S(1)}, s32[1,16]{1,0:T(1,128)}, u32[]{:S(2)}) copy-start(s32[1,16]{1,0:T(1,128)} %param.15) | copy-start | bytes 196
  10.3 100.2 %all-gather.6.cloned.1.call-start = ((), (), s32[]{:S(2)}) async-start(), calls=%async_computation.3 | async-start | bytes 7864320 | tf_op jit(solution)/shard_map/all_gather | solution.py:48
  68.0 1.5 copy-start.3
  68.0 2.1 %copy-start.4 = (s32[1,16]{1,0:T(1,128)S(1)}, s32[1,16]{1,0:T(1,128)}, u32[]{:S(2)}) copy-start(s32[1,16]{1,0:T(1,128)} %param.16) | copy-start | bytes 196
  72.3 4.7 %copy-start.7 = (s32[1,16]{1,0:T(1,128)S(1)}, s32[1,16]{1,0:T(1,128)}, u32[]{:S(2)}) copy-start(s32[1,16]{1,0:T(1,128)} %param.14) | copy-start | bytes 196
  73.4 30.9 %all-to-all-start = ((bf16[16,272,128]{2,1,0:T(8,128)(2,1)}), bf16[16,272,128]{2,1,0:T(8,128)(2,1)S(1)}, u32[]{:S(2)}, u32[]{:S(2)}) async-start(bf16[16,272,128]{2,1,0:T(8,128)(2,1)} %pad_maximum_fusion), calls=%async_computation | async-start | bytes 2228224 | tf_op jit(solution)/shard_map/all_to_all | solution.py:36
  76.9 42.3 %all-gather.8.cloned.1.call-start = ((), (), s32[]{:S(2)}) async-start(), calls=%async_computation.4 | async-start | bytes 3145728 | tf_op jit(solution)/shard_map/all_gather | solution.py:40
  77.0 29.2 %copy-start.6 = (s32[2]{0:T(128)S(1)}, s32[2]{0:T(128)}, u32[]{:S(2)}) copy-start(s32[2]{0:T(128)} %param.18) | copy-start | bytes 28
  105.0 1.5 copy-start.2
Sparse Core Ops, SparseCore 0:
  10.5 57.4 all-gather.3
  69.6 13.9 all-gather.5
  106.3 9.4 all-gather.7

commit v2 on v0

v2 whole, which is shorter than its diff:
```python
import functools

import jax
import jax.numpy as jnp
from jax import lax
from jax.experimental import pallas as pl
from jax.experimental.pallas import tpu as pltpu
from jax.sharding import PartitionSpec as P

BF = jnp.bfloat16
F32 = jnp.float32
MESH = pl.DeviceIdType.MESH


def kernel(
    n,
    mpos,
    send_ref,
    recv_ref,
    pair_ref,
    right_of_ref,
    lsize_ref,
    rsize_ref,
    pattern_ref,
    wf_ref,
    left_ref,
    right_ref,
    out_ref,
    lbuf,
    rbuf,
    stage,
    tagstage,
    wbuf,
    tagbuf,
    total,
    rounded,
    mbuf,
    ls_own,
    ls,
    lr,
    cs,
    cr,
    ws,
    wr,
    vs,
    vr,
    ts,
    tr,
    ms,
    mr,
):
    me = lax.axis_index("sec")
    m = lax.axis_index("mpo")
    c = lax.axis_index("rep")
    other = 1 - c
    lefts, nw, width = left_ref.shape[:3]
    rights = right_ref.shape[0]
    half = wf_ref.shape[2]
    per = wf_ref.shape[0] // n
    part = width // 2
    mrows = width // mpos

    barrier = pltpu.get_barrier_semaphore()
    for t in range(1, n):
        pl.semaphore_signal(
            barrier, inc=1, device_id={"sec": lax.rem(me + t, n)}, device_id_type=MESH
        )
    for t in range(1, mpos):
        pl.semaphore_signal(
            barrier, inc=1, device_id={"mpo": lax.rem(m + t, mpos)}, device_id_type=MESH
        )
    pl.semaphore_signal(barrier, inc=1, device_id={"rep": other}, device_id_type=MESH)

    row = lax.broadcasted_iota(jnp.int32, (width, width), 0)
    hrow = lax.broadcasted_iota(jnp.int32, (width, half), 0)
    hcol = lax.broadcasted_iota(jnp.int32, (width, half), 1) + c * half

    def my_rows(d, l):
        return lbuf.at[d, l, :, pl.ds(pl.multiple_of(c * part, part), part), :]

    def hop(d, l, step, sem):
        return pltpu.make_async_remote_copy(
            src_ref=my_rows(d, l),
            dst_ref=my_rows(d, l),
            send_sem=sem,
            recv_sem=lr.at[d, l],
            device_id={"sec": me + step},
            device_id_type=MESH,
        )

    def cross(d, l):
        return pltpu.make_async_remote_copy(
            src_ref=my_rows(d, l),
            dst_ref=my_rows(d, l),
            send_sem=cs.at[d, l],
            recv_sem=cr.at[d, l],
            device_id={"rep": other},
            device_id_type=MESH,
        )

    def wave(e):
        return pltpu.make_async_remote_copy(
            src_ref=stage.at[e],
            dst_ref=wbuf.at[me, c],
            send_sem=ws.at[e],
            recv_sem=wr.at[me],
            device_id={"sec": e},
            device_id_type=MESH,
        )

    def wave_from(d):
        return pltpu.make_async_remote_copy(
            src_ref=stage.at[d],
            dst_ref=wbuf.at[d, c],
            send_sem=ws.at[d],
            recv_sem=wr.at[d],
            device_id={"sec": d},
            device_id_type=MESH,
        )

    def wave_cross(d, side):
        return pltpu.make_async_remote_copy(
            src_ref=wbuf.at[d, side],
            dst_ref=wbuf.at[d, side],
            send_sem=vs.at[d],
            recv_sem=vr.at[d],
            device_id={"rep": other},
            device_id_type=MESH,
        )

    def tags(e, slot):
        return pltpu.make_async_remote_copy(
            src_ref=tagstage.at[e],
            dst_ref=tagbuf.at[slot],
            send_sem=ts.at[e],
            recv_sem=tr.at[slot],
            device_id={"sec": e},
            device_id_type=MESH,
        )

    def partial_to(d, o):
        target = lax.rem(m + o, mpos)
        rows = pl.ds(pl.multiple_of(target * mrows, mrows), mrows)
        return pltpu.make_async_remote_copy(
            src_ref=rounded.at[d, :, rows, :],
            dst_ref=mbuf.at[o - 1, d],
            send_sem=ms.at[d, o - 1],
            recv_sem=mr.at[d, o - 1],
            device_id={"mpo": target},
            device_id_type=MESH,
        )

    for l in range(lefts):
        size = lsize_ref[l]
        keep = jnp.where(row < size, 1.0, 0.0)
        for w in range(nw):
            scale = (keep * pattern_ref[l, w].astype(F32)).astype(BF)
            lbuf[me, l, w] = left_ref[l, w] * scale
        if l == 0:
            pl.semaphore_wait(barrier, n + mpos - 1)

        @pl.when(me + 1 < n)
        def _():
            hop(me, l, 1, ls_own.at[0, l]).start()

        @pl.when(me > 0)
        def _():
            hop(me, l, -1, ls_own.at[1, l]).start()

    def fill(e, carry):
        for k in range(per):
            block = send_ref[0, e * per + k]
            left = pair_ref[0, block]
            keep = jnp.where(hrow < lsize_ref[left], 1.0, 0.0).astype(BF)
            stage[e, k] = wf_ref[block] * keep
            for l in range(lefts):
                flag = jnp.where(left == l, 1.0, 0.0)
                tagstage[e, k, l] = jnp.full((16, 128), flag, F32).astype(BF)

        @pl.when(e != me)
        def _():
            tags(e, me).start()
            wave(e).start()

        return carry

    lax.fori_loop(0, n, fill, 0)
    wbuf[me, c] = stage[me]
    tagbuf[me] = tagstage[me]
    wave_cross(me, c).start()

    for b in range(rights):
        size = rsize_ref[b]
        keep = jnp.where(jnp.logical_and(hrow < size, hcol < size), 1.0, 0.0).astype(BF)
        for w in range(nw):
            rbuf[b, w] = right_ref[b, w] * keep

    def compute(d):
        def one(k, carry):
            x = jnp.concatenate([wbuf[d, 0, k], wbuf[d, 1, k]], axis=1)
            b = right_of_ref[0, d * per + k]
            flags = []
            for l in range(lefts):
                flag = tagbuf[d, k, l]
                flag = jnp.concatenate([flag] * (width // 128), axis=1)
                flags.append(jnp.concatenate([flag] * (width // 16), axis=0))
            acc = jnp.zeros((width, half), F32)
            for w in range(nw):
                env = lbuf[d, 0, w] * flags[0]
                for l in range(1, lefts):
                    env = env + lbuf[d, l, w] * flags[l]
                y = jnp.dot(env, x, preferred_element_type=F32).astype(BF)
                acc = acc + jnp.dot(y, rbuf[b, w], preferred_element_type=F32)
            total[d, k] = acc
            rounded[d, k] = acc.astype(BF)
            return carry

        lax.fori_loop(0, per, one, 0)
        for o in range(1, mpos):
            partial_to(d, o).start()

    wave_cross(me, other).wait_recv()
    compute(me)

    def arrive(t, carry):
        for l in range(lefts):
            for step in (1, -1):
                d = me - step * t

                @pl.when(jnp.logical_and(d >= 0, d < n))
                def _():
                    if l == 0:
                        tags(d, d).wait_recv()
                        wave_from(d).wait_recv()
                        wave_cross(d, c).start()
                    hop(d, l, -step, ls.at[d, l]).wait_recv()
                    nxt = me + step

                    @pl.when(jnp.logical_and(nxt >= 0, nxt < n))
                    def _():
                        hop(d, l, step, ls.at[d, l]).start()

                    cross(d, l).start()

        return carry

    def finish(t):
        for step in (1, -1):
            d = me - step * t

            @pl.when(jnp.logical_and(d >= 0, d < n))
            def _():
                wave_cross(d, other).wait_recv()
                for l in range(lefts):
                    cross(d, l).wait_recv()
                compute(d)

    def turn(t, carry):
        arrive(t, 0)

        @pl.when(t > 1)
        def _():
            finish(t - 1)

        return carry

    lax.fori_loop(1, n, turn, 0)
    finish(n - 1)

    for l in range(lefts):

        @pl.when(me + 1 < n)
        def _():
            hop(me, l, 1, ls_own.at[0, l]).wait_send()

        @pl.when(me > 0)
        def _():
            hop(me, l, -1, ls_own.at[1, l]).wait_send()

    def drain(d, carry):
        wave_cross(d, c).wait_send()
        for o in range(1, mpos):
            partial_to(d, o).wait()

        @pl.when(d != me)
        def _():
            wave(d).wait_send()
            tags(d, me).wait_send()
            for l in range(lefts):
                cross(d, l).wait_send()

        @pl.when(jnp.logical_and(d < me, me + 1 < n))
        def _():
            for l in range(lefts):
                hop(d, l, 1, ls.at[d, l]).wait_send()

        @pl.when(jnp.logical_and(d > me, me > 0))
        def _():
            for l in range(lefts):
                hop(d, l, -1, ls.at[d, l]).wait_send()

        return carry

    lax.fori_loop(0, n, drain, 0)

    own = pl.ds(pl.multiple_of(m * mrows, mrows), mrows)

    def emit(i, carry):
        r = recv_ref[0, i]
        d, k = r // per, lax.rem(r, per)
        value = total[d, k, own, :]
        for o in range(1, mpos):
            value = value + mbuf[o - 1, d, k].astype(F32)
        out_ref[i] = value.astype(BF)
        return carry

    lax.fori_loop(0, n * per, emit, 0)


def local(
    n,
    mpos,
    wavefunction,
    left_env,
    right_env,
    send_order,
    recv_order,
    pair_left,
    pair_right,
    left_size,
    right_size,
    mpo_pattern,
):
    pairs, width, half = wavefunction.shape
    per = pairs // n
    lefts, nw = left_env.shape[:2]
    slots = jnp.arange(pairs, dtype=jnp.int32)
    match = recv_order[0][None, :] == slots[:, None]
    right_of = jnp.sum(jnp.where(match, pair_right[0][None, :], 0), axis=1)[None, :]
    smem = pl.BlockSpec(memory_space=pltpu.SMEM)
    vmem = pl.BlockSpec(memory_space=pltpu.VMEM)
    dma = pltpu.SemaphoreType.DMA
    others = max(mpos - 1, 1)
    return pl.pallas_call(
        functools.partial(kernel, n, mpos),
        out_shape=jax.ShapeDtypeStruct((pairs, width // mpos, half), BF),
        in_specs=[smem] * 7 + [vmem] * 3,
        out_specs=vmem,
        scratch_shapes=[
            pltpu.VMEM((n, lefts, nw, width, width), BF),
            pltpu.VMEM(right_env.shape, BF),
            pltpu.VMEM((n, per, width, half), BF),
            pltpu.VMEM((n, per, lefts, 16, 128), BF),
            pltpu.VMEM((n, 2, per, width, half), BF),
            pltpu.VMEM((n, per, lefts, 16, 128), BF),
            pltpu.VMEM((n, per, width, half), F32),
            pltpu.VMEM((n, per, width, half), BF),
            pltpu.VMEM((others, n, per, width // mpos, half), BF),
            dma((2, lefts)),
            dma((n, lefts)),
            dma((n, lefts)),
            dma((n, lefts)),
            dma((n, lefts)),
            dma((n,)),
            dma((n,)),
            dma((n,)),
            dma((n,)),
            dma((n,)),
            dma((n,)),
            dma((n, others)),
            dma((n, others)),
        ],
        compiler_params=pltpu.CompilerParams(
            collective_id=0, has_side_effects=True, vmem_limit_bytes=52 * 1024 * 1024
        ),
        cost_estimate=pl.CostEstimate(
            flops=6 * pairs * nw * width * width * half,
            bytes_accessed=8 * pairs * width * half,
            transcendentals=0,
        ),
        name="apply_blocks",
    )(
        send_order,
        recv_order,
        pair_left,
        right_of,
        left_size,
        right_size,
        mpo_pattern,
        wavefunction,
        left_env,
        right_env,
    )


def solution(mesh):
    placed = (
        P(("runs", "sec"), None, "rep"),
        P(("runs", "sec"), "mpo", None, None),
        P(("runs", "sec"), "mpo", None, "rep"),
        P("sec", None),
        P("sec", None),
        P("sec", None),
        P("sec", None),
        P("sec"),
        P("sec"),
        P("sec", "mpo"),
    )
    return jax.shard_map(
        functools.partial(local, mesh.shape["sec"], mesh.shape["mpo"]),
        mesh=mesh,
        in_specs=placed,
        out_specs=P(("runs", "sec"), "mpo", "rep"),
        check_vma=False,
    )
```

time: 327 us -> 93.3 us (0.29)
  waiting for transfers between devices: 259 us -> 0 us
  Pallas kernels: 0 us -> 86.4 us
  local copies, waits for them, and re-layouts: 24.9 us -> 5.83 us
  matrix products: 18 us -> 0 us
  between operations: 13.5 us -> 0.02 us
  starting transfers between devices: 6.16 us -> 0 us
  other arithmetic: 5.66 us -> 0.79 us
    all_to_all x1 -> x0, waiting for transfers between devices: 223 us -> none  [local(): lax.all_to_all(outgoing, 'sec', split_axis=0, concat_axis=0, tiled=True)]
    pallas_call x0 -> x1, Pallas kernels: none -> 86.4 us  [local(): pl.pallas_call(functools.partial(kernel, n, mpos), out_shape=jax.ShapeDty...]
    reduce_scatter x1 -> x0, waiting for transfers between devices: 31.3 us -> none  [local(): lax.psum_scatter(partial_value, 'mpo', scatter_dimension=1, tiled=True)]
    gather x8 -> x0, local copies, waits for them, and re-layouts: 24.9 us -> none  [the longest x1 9.57 us: local(): arrived = arrived.reshape(interim.shape)[recv_order[0]]]
    dot_general x2 -> x0, matrix products: 18 us -> none  [the longest x1 9.77 us: local(): jnp.einsum('pwik,pwkj->pij', arrived, right_blocks, preferred_element_typ...]
    all_to_all x1 -> x0, starting transfers between devices: 6.12 us -> none  [local(): lax.all_to_all(outgoing, 'sec', split_axis=0, concat_axis=0, tiled=True)]
    unnamed x12 -> x15, local copies, waits for them, and re-layouts: 0.03 us -> 5.83 us
    all_gather x1 -> x0, waiting for transfers between devices: 3.67 us -> none  [local(): source = lax.all_gather(wavefunction, 'rep', axis=2, tiled=True)]
  transfers between devices with their start and end apart: 3 -> 0, of which waited for: 3 -> 0; matrix products, arithmetic and copies ran while one was open for 5% -> 0% of each run, Pallas kernels for 0% -> 0%
where the time goes in v2:
time: 93.3 us; the launch traced here: 93.1 us
  Pallas kernels  86.4 us (93%)
  local copies, waits for them, and re-layouts  5.83 us (6%)
    pallas_call x1, Pallas kernels, local(): pl.pallas_call(functools.partial(kernel, n, mpos), out_shape=jax.ShapeDty...  86.4 us
    unnamed x15, local copies, waits for them, and re-layouts  5.83 us

profile of v2, /device:TPU:0, one launch (start us, length us, event | category | flops | bytes accessed | tf_op | source)
XLA Modules:
  0.0 93.1 jit_solution(15001515602304263162)
XLA Ops:
  0.0 0.8 select_reduce_fusion
  0.8 0.0 copy-start
  0.8 1.1 %copy-done = bf16[2,5,256,128]{3,2,1,0:T(8,128)(2,1)S(1)} copy-done((bf16[2,5,256,128]{3,2,1,0:T(8,128)(2,1)S(1)}, bf16[2,5,256,128]{3,2,1,0:T(8,128)(2,1)}, u32[]{:S(2)}) %copy-start) | copy-done | bytes 655384
  1.9 0.0 copy-start.1
  1.9 0.7 copy-done.1
  2.6 0.0 copy-start.2
  2.6 0.7 copy-done.2
  3.2 0.0 copy-start.3
  3.2 0.7 copy-done.3
  3.9 0.0 copy-start.4
  3.9 0.7 copy-done.4
  4.5 0.0 copy-start.5
  4.5 0.7 copy-done.5
  5.2 0.0 copy-start.6
  5.2 0.7 copy-done.6
  5.8 86.4 %apply_blocks.1 = bf16[16,128,128]{2,1,0:T(8,128)(2,1)S(1)} custom-call(s32[1,16]{1,0:T(1,128)S(1)} %copy-done.2, s32[1,16]{1,0:T(1,128)S(1)} %copy-done.3, s32[1,16]{1,0:T(1,128)S(1)} %copy-done.4, s32[1,16]{1,0:T(1,128)S(1)} %bitcast.4, s32[2]{0:T(128)S(1)} %copy-done.5, s32[2]{0:T(128)S(1)} %copy-done.6, s32[2,5]{1,0:T(2,128)S(1)} %copy-done.1, ...), custom_call_target="tpu_custom_call" | custom-call | flops 4026531840 | bytes 4194304 | tf_op jit(solution)/shard_map/apply_blocks/pallas_call | solution.py:344
  92.3 0.8 copy.12
Async XLA Ops:
  0.8 1.1 %copy-start = (bf16[2,5,256,128]{3,2,1,0:T(8,128)(2,1)S(1)}, bf16[2,5,256,128]{3,2,1,0:T(8,128)(2,1)}, u32[]{:S(2)}) copy-start(bf16[2,5,256,128]{3,2,1,0:T(8,128)(2,1)} %right_ref.1) | copy-start | bytes 1966084
  1.9 0.7 copy-start.1
  2.6 0.7 copy-start.2
  3.2 0.7 copy-start.3
  3.9 0.7 copy-start.4
  4.5 0.7 copy-start.5
  5.2 0.7 copy-start.6

commit v3 on v2

--- a/solution.py
+++ b/solution.py
@@ -22,10 +22,14 @@
     lsize_ref,
     rsize_ref,
     pattern_ref,
+    wf_hbm,
+    left_hbm,
+    right_hbm,
+    out_ref,
     wf_ref,
     left_ref,
     right_ref,
-    out_ref,
+    load,
     lbuf,
     rbuf,
     stage,
@@ -42,6 +46,8 @@
     cr,
     ws,
     wr,
+    xs,
+    xr,
     vs,
     vr,
     ts,
@@ -60,6 +66,12 @@
     part = width // 2
     mrows = width // mpos
 
+    load_left = pltpu.make_async_copy(left_hbm, left_ref, load.at[0])
+    load_wf = pltpu.make_async_copy(wf_hbm, wf_ref, load.at[1])
+    load_right = pltpu.make_async_copy(right_hbm, right_ref, load.at[2])
+    load_left.start()
+    load_wf.start()
+    load_right.start()
     barrier = pltpu.get_barrier_semaphore()
     for t in range(1, n):
         pl.semaphore_signal(
@@ -75,46 +87,60 @@
     hrow = lax.broadcasted_iota(jnp.int32, (width, half), 0)
     hcol = lax.broadcasted_iota(jnp.int32, (width, half), 1) + c * half
 
-    def my_rows(d, l):
-        return lbuf.at[d, l, :, pl.ds(pl.multiple_of(c * part, part), part), :]
-
-    def hop(d, l, step, sem):
-        return pltpu.make_async_remote_copy(
-            src_ref=my_rows(d, l),
-            dst_ref=my_rows(d, l),
+    def my_rows(d, q):
+        return lbuf.at[d, q, :, pl.ds(pl.multiple_of(c * part, part), part), :]
+
+    def hop(d, q, step, sem):
+        return pltpu.make_async_remote_copy(
+            src_ref=my_rows(d, q),
+            dst_ref=my_rows(d, q),
             send_sem=sem,
-            recv_sem=lr.at[d, l],
+            recv_sem=lr.at[d, q],
             device_id={"sec": me + step},
             device_id_type=MESH,
         )
 
-    def cross(d, l):
-        return pltpu.make_async_remote_copy(
-            src_ref=my_rows(d, l),
-            dst_ref=my_rows(d, l),
-            send_sem=cs.at[d, l],
-            recv_sem=cr.at[d, l],
+    def cross(d, q):
+        return pltpu.make_async_remote_copy(
+            src_ref=my_rows(d, q),
+            dst_ref=my_rows(d, q),
+            send_sem=cs.at[d, q],
+            recv_sem=cr.at[d, q],
             device_id={"rep": other},
             device_id_type=MESH,
         )
 
-    def wave(e):
-        return pltpu.make_async_remote_copy(
-            src_ref=stage.at[e],
-            dst_ref=wbuf.at[me, c],
+    own = pl.ds(pl.multiple_of(m * mrows, mrows), mrows)
+
+    def wave(e, slot):
+        return pltpu.make_async_remote_copy(
+            src_ref=stage.at[e, :, own, :],
+            dst_ref=wbuf.at[slot, c, :, own, :],
             send_sem=ws.at[e],
-            recv_sem=wr.at[me],
+            recv_sem=wr.at[slot],
             device_id={"sec": e},
             device_id_type=MESH,
         )
 
-    def wave_from(d):
-        return pltpu.make_async_remote_copy(
-            src_ref=stage.at[d],
-            dst_ref=wbuf.at[d, c],
-            send_sem=ws.at[d],
-            recv_sem=wr.at[d],
-            device_id={"sec": d},
+    def wave_share(d, o):
+        return pltpu.make_async_remote_copy(
+            src_ref=wbuf.at[d, c, :, own, :],
+            dst_ref=wbuf.at[d, c, :, own, :],
+            send_sem=xs.at[d, o - 1],
+            recv_sem=xr.at[d, o - 1],
+            device_id={"mpo": lax.rem(m + o, mpos)},
+            device_id_type=MESH,
+        )
+
+    def wave_shared(d, o):
+        source = lax.rem(m + mpos - o, mpos)
+        rows = pl.ds(pl.multiple_of(source * mrows, mrows), mrows)
+        return pltpu.make_async_remote_copy(
+            src_ref=wbuf.at[d, c, :, rows, :],
+            dst_ref=wbuf.at[d, c, :, rows, :],
+            send_sem=xs.at[d, o - 1],
+            recv_sem=xr.at[d, o - 1],
+            device_id={"mpo": source},
             device_id_type=MESH,
         )
 
@@ -150,22 +176,24 @@
             device_id_type=MESH,
         )
 
-    for l in range(lefts):
-        size = lsize_ref[l]
-        keep = jnp.where(row < size, 1.0, 0.0)
-        for w in range(nw):
-            scale = (keep * pattern_ref[l, w].astype(F32)).astype(BF)
-            lbuf[me, l, w] = left_ref[l, w] * scale
-        if l == 0:
+    keeps = [jnp.where(row < lsize_ref[l], 1.0, 0.0) for l in range(lefts)]
+    load_left.wait()
+    for q in range(nw):
+        for l in range(lefts):
+            scale = (keeps[l] * pattern_ref[l, q].astype(F32)).astype(BF)
+            lbuf[me, q, l] = left_ref[l, q] * scale
+        if q == 0:
             pl.semaphore_wait(barrier, n + mpos - 1)
 
         @pl.when(me + 1 < n)
         def _():
-            hop(me, l, 1, ls_own.at[0, l]).start()
+            hop(me, q, 1, ls_own.at[0, q]).start()
 
         @pl.when(me > 0)
         def _():
-            hop(me, l, -1, ls_own.at[1, l]).start()
+            hop(me, q, -1, ls_own.at[1, q]).start()
+
+    load_wf.wait()
 
     def fill(e, carry):
         for k in range(per):
@@ -180,7 +208,7 @@
         @pl.when(e != me)
         def _():
             tags(e, me).start()
-            wave(e).start()
+            wave(e, me).start()
 
         return carry
 
@@ -189,93 +217,109 @@
     tagbuf[me] = tagstage[me]
     wave_cross(me, c).start()
 
+    load_right.wait()
     for b in range(rights):
         size = rsize_ref[b]
         keep = jnp.where(jnp.logical_and(hrow < size, hcol < size), 1.0, 0.0).astype(BF)
         for w in range(nw):
             rbuf[b, w] = right_ref[b, w] * keep
 
-    def compute(d):
-        def one(k, carry):
+    def compute(d, q):
+        for k in range(per):
             x = jnp.concatenate([wbuf[d, 0, k], wbuf[d, 1, k]], axis=1)
             b = right_of_ref[0, d * per + k]
-            flags = []
+            env = None
             for l in range(lefts):
                 flag = tagbuf[d, k, l]
                 flag = jnp.concatenate([flag] * (width // 128), axis=1)
-                flags.append(jnp.concatenate([flag] * (width // 16), axis=0))
-            acc = jnp.zeros((width, half), F32)
-            for w in range(nw):
-                env = lbuf[d, 0, w] * flags[0]
-                for l in range(1, lefts):
-                    env = env + lbuf[d, l, w] * flags[l]
-                y = jnp.dot(env, x, preferred_element_type=F32).astype(BF)
-                acc = acc + jnp.dot(y, rbuf[b, w], preferred_element_type=F32)
-            total[d, k] = acc
-            rounded[d, k] = acc.astype(BF)
-            return carry
-
-        lax.fori_loop(0, per, one, 0)
-        for o in range(1, mpos):
-            partial_to(d, o).start()
+                flag = jnp.concatenate([flag] * (width // 16), axis=0)
+                term = lbuf[d, q, l] * flag
+                env = term if env is None else env + term
+            y = jnp.dot(env, x, preferred_element_type=F32).astype(BF)
+            total[d, k] += jnp.dot(y, rbuf[b, q], preferred_element_type=F32)
+
+        @pl.when(q == nw - 1)
+        def _():
+            for k in range(per):
+                rounded[d, k] = total[d, k].astype(BF)
+            for o in range(1, mpos):
+                partial_to(d, o).start()
+
+    def clear(d, carry):
+        for k in range(per):
+            total[d, k] = jnp.zeros((width, half), F32)
+        return carry
+
+    lax.fori_loop(0, n, clear, 0)
 
     wave_cross(me, other).wait_recv()
-    compute(me)
-
-    def arrive(t, carry):
-        for l in range(lefts):
-            for step in (1, -1):
-                d = me - step * t
-
-                @pl.when(jnp.logical_and(d >= 0, d < n))
-                def _():
-                    if l == 0:
-                        tags(d, d).wait_recv()
-                        wave_from(d).wait_recv()
-                        wave_cross(d, c).start()
-                    hop(d, l, -step, ls.at[d, l]).wait_recv()
-                    nxt = me + step
-
-                    @pl.when(jnp.logical_and(nxt >= 0, nxt < n))
-                    def _():
-                        hop(d, l, step, ls.at[d, l]).start()
-
-                    cross(d, l).start()
-
-        return carry
-
-    def finish(t):
+
+    def first(q, carry):
+        compute(me, q)
+        return carry
+
+    lax.fori_loop(0, nw, first, 0)
+
+    def arrive(t, q):
         for step in (1, -1):
             d = me - step * t
 
             @pl.when(jnp.logical_and(d >= 0, d < n))
             def _():
-                wave_cross(d, other).wait_recv()
-                for l in range(lefts):
-                    cross(d, l).wait_recv()
-                compute(d)
-
-    def turn(t, carry):
-        arrive(t, 0)
-
-        @pl.when(t > 1)
-        def _():
-            finish(t - 1)
-
-        return carry
-
-    lax.fori_loop(1, n, turn, 0)
-    finish(n - 1)
-
-    for l in range(lefts):
+                hop(d, q, -step, ls.at[d, q]).wait_recv()
+                nxt = me + step
+
+                @pl.when(jnp.logical_and(nxt >= 0, nxt < n))
+                def _():
+                    hop(d, q, step, ls.at[d, q]).start()
+
+                cross(d, q).start()
+
+                @pl.when(q == 0)
+                def _():
+                    tags(d, d).wait_recv()
+                    wave(d, d).wait_recv()
+                    for o in range(1, mpos):
+                        wave_share(d, o).start()
+                    for o in range(1, mpos):
+                        wave_shared(d, o).wait_recv()
+                    wave_cross(d, c).start()
+
+    def finish(t, q):
+        for step in (1, -1):
+            d = me - step * t
+
+            @pl.when(jnp.logical_and(d >= 0, d < n))
+            def _():
+                @pl.when(q == 0)
+                def _():
+                    wave_cross(d, other).wait_recv()
+
+                cross(d, q).wait_recv()
+                compute(d, q)
+
+    def turn(u, carry):
+        @pl.when(u < (n - 1) * nw)
+        def _():
+            arrive(u // nw + 1, lax.rem(u, nw))
+
+        @pl.when(u > 0)
+        def _():
+            finish((u - 1) // nw + 1, lax.rem(u + nw - 1, nw))
+
+        return carry
+
+    lax.fori_loop(0, (n - 1) * nw + 1, turn, 0)
+
+    for q in range(nw):
 
         @pl.when(me + 1 < n)
         def _():
-            hop(me, l, 1, ls_own.at[0, l]).wait_send()
+            hop(me, q, 1, ls_own.at[0, q]).wait_send()
 
         @pl.when(me > 0)
         def _():
-            hop(me, l, -1, ls_own.at[1, l]).wait_send()
+            hop(me, q, -1, ls_own.at[1, q]).wait_send()
 
     def drain(d, carry):
         wave_cross(d, c).wait_send()
@@ -284,26 +328,26 @@
 
         @pl.when(d != me)
         def _():
-            wave(d).wait_send()
+            wave(d, me).wait_send()
+            for o in range(1, mpos):
+                wave_share(d, o).wait_send()
             tags(d, me).wait_send()
-            for l in range(lefts):
-                cross(d, l).wait_send()
+            for q in range(nw):
+                cross(d, q).wait_send()
 
         @pl.when(jnp.logical_and(d < me, me + 1 < n))
         def _():
-            for l in range(lefts):
-                hop(d, l, 1, ls.at[d, l]).wait_send()
+            for q in range(nw):
+                hop(d, q, 1, ls.at[d, q]).wait_send()
 
         @pl.when(jnp.logical_and(d > me, me > 0))
         def _():
-            for l in range(lefts):
-                hop(d, l, -1, ls.at[d, l]).wait_send()
+            for q in range(nw):
+                hop(d, q, -1, ls.at[d, q]).wait_send()
 
         return carry
 
     lax.fori_loop(0, n, drain, 0)
-
-    own = pl.ds(pl.multiple_of(m * mrows, mrows), mrows)
 
     def emit(i, carry):
         r = recv_ref[0, i]
@@ -344,10 +388,14 @@
     return pl.pallas_call(
         functools.partial(kernel, n, mpos),
         out_shape=jax.ShapeDtypeStruct((pairs, width // mpos, half), BF),
-        in_specs=[smem] * 7 + [vmem] * 3,
+        in_specs=[smem] * 7 + [pl.BlockSpec(memory_space=pl.ANY)] * 3,
         out_specs=vmem,
         scratch_shapes=[
-            pltpu.VMEM((n, lefts, nw, width, width), BF),
+            pltpu.VMEM(wavefunction.shape, BF),
+            pltpu.VMEM(left_env.shape, BF),
+            pltpu.VMEM(right_env.shape, BF),
+            dma((3,)),
+            pltpu.VMEM((n, nw, lefts, width, width), BF),
             pltpu.VMEM(right_env.shape, BF),
             pltpu.VMEM((n, per, width, half), BF),
             pltpu.VMEM((n, per, lefts, 16, 128), BF),
@@ -356,13 +404,15 @@
             pltpu.VMEM((n, per, width, half), F32),
             pltpu.VMEM((n, per, width, half), BF),
             pltpu.VMEM((others, n, per, width // mpos, half), BF),
-            dma((2, lefts)),
-            dma((n, lefts)),
-            dma((n, lefts)),
-            dma((n, lefts)),
-            dma((n, lefts)),
-            dma((n,)),
-            dma((n,)),
+            dma((2, nw)),
+            dma((n, nw)),
+            dma((n, nw)),
+            dma((n, nw)),
+            dma((n, nw)),
+            dma((n,)),
+            dma((n,)),
+            dma((n, others)),
+            dma((n, others)),
             dma((n,)),
             dma((n,)),
             dma((n,)),

time: 93.3 us -> 81.1 us (0.87)
  Pallas kernels: 86.4 us -> 74.2 us
    pallas_call x1, Pallas kernels: 86.4 us -> 74.2 us  [local(): pl.pallas_call(functools.partial(kernel, n, mpos), out_shape=jax.ShapeDty...]
where the time goes in v3:
time: 81.1 us; the launch traced here: 80.9 us
  Pallas kernels  74.2 us (91%)
  local copies, waits for them, and re-layouts  5.83 us (7%)
    pallas_call x1, Pallas kernels, local(): pl.pallas_call(functools.partial(kernel, n, mpos), out_shape=jax.ShapeDty...  74.2 us
    unnamed x15, local copies, waits for them, and re-layouts  5.83 us

profile of v3, /device:TPU:0, one launch (start us, length us, event | category | flops | bytes accessed | tf_op | source)
XLA Modules:
  0.0 80.9 jit_solution(15158243358372936835)
XLA Ops:
  0.0 0.8 select_reduce_fusion
  0.8 0.0 copy-start
  0.8 1.1 %copy-done = bf16[2,5,256,128]{3,2,1,0:T(8,128)(2,1)S(1)} copy-done((bf16[2,5,256,128]{3,2,1,0:T(8,128)(2,1)S(1)}, bf16[2,5,256,128]{3,2,1,0:T(8,128)(2,1)}, u32[]{:S(2)}) %copy-start) | copy-done | bytes 655384
  1.9 0.0 copy-start.1
  1.9 0.7 copy-done.1
  2.6 0.0 copy-start.2
  2.6 0.7 copy-done.2
  3.2 0.0 copy-start.3
  3.2 0.7 copy-done.3
  3.9 0.0 copy-start.4
  3.9 0.7 copy-done.4
  4.5 0.0 copy-start.5
  4.5 0.7 copy-done.5
  5.2 0.0 copy-start.6
  5.2 0.7 copy-done.6
  5.8 74.2 %apply_blocks.1 = bf16[16,128,128]{2,1,0:T(8,128)(2,1)S(1)} custom-call(s32[1,16]{1,0:T(1,128)S(1)} %copy-done.2, s32[1,16]{1,0:T(1,128)S(1)} %copy-done.3, s32[1,16]{1,0:T(1,128)S(1)} %copy-done.4, s32[1,16]{1,0:T(1,128)S(1)} %bitcast.4, s32[2]{0:T(128)S(1)} %copy-done.5, s32[2]{0:T(128)S(1)} %copy-done.6, s32[2,5]{1,0:T(2,128)S(1)} %copy-done.1, ...), custom_call_target="tpu_custom_call" | custom-call | flops 4026531840 | bytes 4194304 | tf_op jit(solution)/shard_map/apply_blocks/pallas_call | solution.py:388
  80.1 0.8 copy.12
Async XLA Ops:
  0.8 1.1 %copy-start = (bf16[2,5,256,128]{3,2,1,0:T(8,128)(2,1)S(1)}, bf16[2,5,256,128]{3,2,1,0:T(8,128)(2,1)}, u32[]{:S(2)}) copy-start(bf16[2,5,256,128]{3,2,1,0:T(8,128)(2,1)} %right_hbm.1) | copy-start | bytes 1966084
  1.9 0.7 copy-start.1
  2.6 0.7 copy-start.2
  3.2 0.7 copy-start.3
  3.9 0.7 copy-start.4
  4.5 0.7 copy-start.5
  5.2 0.7 copy-start.6

commit v4 on v3

--- a/solution.py
+++ b/solution.py
@@ -15,13 +15,13 @@
 def kernel(
     n,
     mpos,
-    send_ref,
-    recv_ref,
-    pair_ref,
-    right_of_ref,
-    lsize_ref,
-    rsize_ref,
-    pattern_ref,
+    send_hbm,
+    recv_hbm,
+    pair_hbm,
+    pair_right_hbm,
+    lsize_hbm,
+    rsize_hbm,
+    pattern_hbm,
     wf_hbm,
     left_hbm,
     right_hbm,
@@ -30,6 +30,15 @@
     left_ref,
     right_ref,
     load,
+    send_ref,
+    recv_ref,
+    pair_ref,
+    pair_right_ref,
+    lsize_ref,
+    rsize_ref,
+    pattern_ref,
+    right_of_ref,
+    load_small,
     lbuf,
     rbuf,
     stage,
@@ -69,6 +78,18 @@
     load_left = pltpu.make_async_copy(left_hbm, left_ref, load.at[0])
     load_wf = pltpu.make_async_copy(wf_hbm, wf_ref, load.at[1])
     load_right = pltpu.make_async_copy(right_hbm, right_ref, load.at[2])
+    smalls = (
+        (lsize_hbm, lsize_ref),
+        (pattern_hbm, pattern_ref),
+        (send_hbm, send_ref),
+        (pair_hbm, pair_ref),
+        (recv_hbm, recv_ref),
+        (pair_right_hbm, pair_right_ref),
+        (rsize_hbm, rsize_ref),
+    )
+    small = [pltpu.make_async_copy(a, b, load_small.at[i]) for i, (a, b) in enumerate(smalls)]
+    for copy in small:
+        copy.start()
     load_left.start()
     load_wf.start()
     load_right.start()
@@ -176,6 +197,8 @@
             device_id_type=MESH,
         )
 
+    for copy in small:
+        copy.wait()
     keeps = [jnp.where(row < lsize_ref[l], 1.0, 0.0) for l in range(lefts)]
     load_left.wait()
     for q in range(nw):
@@ -217,6 +240,15 @@
     tagbuf[me] = tagstage[me]
     wave_cross(me, c).start()
 
+    def invert(r, carry):
+        b = jnp.int32(0)
+        for i in range(n * per):
+            b = jnp.where(recv_ref[0, i] == r, pair_right_ref[0, i], b)
+        right_of_ref[r] = b
+        return carry
+
+    lax.fori_loop(0, n * per, invert, 0)
+
     load_right.wait()
     for b in range(rights):
         size = rsize_ref[b]
@@ -227,7 +259,7 @@
     def compute(d, q):
         for k in range(per):
             x = jnp.concatenate([wbuf[d, 0, k], wbuf[d, 1, k]], axis=1)
-            b = right_of_ref[0, d * per + k]
+            b = right_of_ref[d * per + k]
             env = None
             for l in range(lefts):
                 flag = tagbuf[d, k, l]
@@ -378,23 +410,28 @@
     pairs, width, half = wavefunction.shape
     per = pairs // n
     lefts, nw = left_env.shape[:2]
-    slots = jnp.arange(pairs, dtype=jnp.int32)
-    match = recv_order[0][None, :] == slots[:, None]
-    right_of = jnp.sum(jnp.where(match, pair_right[0][None, :], 0), axis=1)[None, :]
-    smem = pl.BlockSpec(memory_space=pltpu.SMEM)
     vmem = pl.BlockSpec(memory_space=pltpu.VMEM)
     dma = pltpu.SemaphoreType.DMA
     others = max(mpos - 1, 1)
     return pl.pallas_call(
         functools.partial(kernel, n, mpos),
         out_shape=jax.ShapeDtypeStruct((pairs, width // mpos, half), BF),
-        in_specs=[smem] * 7 + [pl.BlockSpec(memory_space=pl.ANY)] * 3,
+        in_specs=[pl.BlockSpec(memory_space=pl.ANY)] * 10,
         out_specs=vmem,
         scratch_shapes=[
             pltpu.VMEM(wavefunction.shape, BF),
             pltpu.VMEM(left_env.shape, BF),
             pltpu.VMEM(right_env.shape, BF),
             dma((3,)),
+            pltpu.SMEM(send_order.shape, jnp.int32),
+            pltpu.SMEM(recv_order.shape, jnp.int32),
+            pltpu.SMEM(pair_left.shape, jnp.int32),
+            pltpu.SMEM(pair_right.shape, jnp.int32),
+            pltpu.SMEM(left_size.shape, jnp.int32),
+            pltpu.SMEM(right_size.shape, jnp.int32),
+            pltpu.SMEM(mpo_pattern.shape, jnp.int32),
+            pltpu.SMEM((pairs,), jnp.int32),
+            dma((7,)),
             pltpu.VMEM((n, nw, lefts, width, width), BF),
             pltpu.VMEM(right_env.shape, BF),
             pltpu.VMEM((n, per, width, half), BF),
@@ -433,7 +470,7 @@
         send_order,
         recv_order,
         pair_left,
-        right_of,
+        pair_right,
         left_size,
         right_size,
         mpo_pattern,

time: 81.1 us -> 80.5 us (level)
    unnamed x15 -> x17, local copies, waits for them, and re-layouts: 5.83 us -> 6.49 us
where the time goes in v4:
time: 80.5 us; the launch traced here: 80.2 us
  Pallas kernels  73.7 us (92%)
  local copies, waits for them, and re-layouts  6.49 us (8%)
    pallas_call x1, Pallas kernels, local(): pl.pallas_call(functools.partial(kernel, n, mpos), out_shape=jax.ShapeDty...  73.7 us
    unnamed x17, local copies, waits for them, and re-layouts  6.49 us

profile of v4, /device:TPU:0, one launch (start us, length us, event | category | flops | bytes accessed | tf_op | source)
XLA Modules:
  0.0 80.2 jit_solution(15025906486250013868)
XLA Ops:
  0.0 0.0 copy-start
  0.0 1.1 %copy-done = bf16[2,5,256,128]{3,2,1,0:T(8,128)(2,1)S(1)} copy-done((bf16[2,5,256,128]{3,2,1,0:T(8,128)(2,1)S(1)}, bf16[2,5,256,128]{3,2,1,0:T(8,128)(2,1)}, u32[]{:S(2)}) %copy-start) | copy-done | bytes 655384
  1.1 0.0 copy-start.1
  1.1 0.7 copy-done.1
  1.8 0.0 copy-start.2
  1.8 0.7 copy-done.2
  2.4 0.0 copy-start.3
  2.4 0.7 copy-done.3
  3.1 0.0 copy-start.4
  3.1 0.7 copy-done.4
  3.7 0.0 copy-start.5
  3.7 0.7 copy-done.5
  4.4 0.0 copy-start.6
  4.4 0.7 copy-done.6
  5.0 0.0 copy-start.7
  5.0 0.7 copy-done.7
  5.7 73.7 %apply_blocks.1 = bf16[16,128,128]{2,1,0:T(8,128)(2,1)S(1)} custom-call(s32[1,16]{1,0:T(1,128)S(1)} %copy-done.2, s32[1,16]{1,0:T(1,128)S(1)} %copy-done.3, s32[1,16]{1,0:T(1,128)S(1)} %copy-done.4, s32[1,16]{1,0:T(1,128)S(1)} %copy-done.5, s32[2]{0:T(128)S(1)} %copy-done.6, s32[2]{0:T(128)S(1)} %copy-done.7, s32[2,5]{1,0:T(2,128)S(1)} %copy-done.1, ...), custom_call_target="tpu_custom_call" | custom-call | flops 4026531840 | bytes 4194304 | tf_op jit(solution)/shard_map/apply_blocks/pallas_call | solution.py:416
  79.4 0.8 copy.12
Async XLA Ops:
  0.0 1.1 %copy-start = (bf16[2,5,256,128]{3,2,1,0:T(8,128)(2,1)S(1)}, bf16[2,5,256,128]{3,2,1,0:T(8,128)(2,1)}, u32[]{:S(2)}) copy-start(bf16[2,5,256,128]{3,2,1,0:T(8,128)(2,1)} %right_hbm.1) | copy-start | bytes 1966084
  1.1 0.7 copy-start.1
  1.8 0.7 copy-start.2
  2.4 0.7 copy-start.3
  3.1 0.7 copy-start.4
  3.7 0.7 copy-start.5
  4.4 0.7 copy-start.6
  5.0 0.7 copy-start.7

commit v5 on v4

--- a/solution.py
+++ b/solution.py
@@ -63,11 +63,35 @@
     tr,
     ms,
     mr,
+    rx,
+    rtagstage,
+    rtag,
+    fstage,
+    fbuf,
+    es,
+    er,
 ):
     me = lax.axis_index("sec")
     m = lax.axis_index("mpo")
     c = lax.axis_index("rep")
     other = 1 - c
+    last = n - 1
+    proxied = n >= 4
+    is_end = jnp.logical_or(me == 0, me == last)
+    is_proxy = jnp.logical_or(me == 1, me == last - 1)
+    helper = jnp.where(me == 0, 1, last - 1)
+    end = jnp.where(me == 1, 0, last)
+    far = last - jnp.where(is_end, me, end)
+
+    def moved(d, e):
+        if not proxied:
+            return d < 0
+        low = jnp.logical_and(d == last, e == 0)
+        return jnp.logical_or(low, jnp.logical_and(d == 0, e == last))
+
+    def both(*terms):
+        return functools.reduce(jnp.logical_and, terms)
+
     lefts, nw, width = left_ref.shape[:3]
     rights = right_ref.shape[0]
     half = wf_ref.shape[2]
@@ -133,13 +157,13 @@
 
     own = pl.ds(pl.multiple_of(m * mrows, mrows), mrows)
 
-    def wave(e, slot):
+    def wave(e, slot, device):
         return pltpu.make_async_remote_copy(
             src_ref=stage.at[e, :, own, :],
             dst_ref=wbuf.at[slot, c, :, own, :],
             send_sem=ws.at[e],
             recv_sem=wr.at[slot],
-            device_id={"sec": e},
+            device_id={"sec": device},
             device_id_type=MESH,
         )
 
@@ -175,13 +199,13 @@
             device_id_type=MESH,
         )
 
-    def tags(e, slot):
+    def tags(e, slot, device):
         return pltpu.make_async_remote_copy(
             src_ref=tagstage.at[e],
             dst_ref=tagbuf.at[slot],
             send_sem=ts.at[e],
             recv_sem=tr.at[slot],
-            device_id={"sec": e},
+            device_id={"sec": device},
             device_id_type=MESH,
         )
 
@@ -230,8 +254,11 @@
 
         @pl.when(e != me)
         def _():
-            tags(e, me).start()
-            wave(e, me).start()
+            away = moved(me, e)
+            slot = jnp.where(away, n, me)
+            device = jnp.where(away, jnp.where(e == 0, 1, last - 1), e)
+            tags(e, slot, device).start()
+            wave(e, slot, device).start()
 
         return carry
 
@@ -255,6 +282,57 @@
         keep = jnp.where(jnp.logical_and(hrow < size, hcol < size), 1.0, 0.0).astype(BF)
         for w in range(nw):
             rbuf[b, w] = right_ref[b, w] * keep
+
+    def to_helper(i, source, target, device):
+        return pltpu.make_async_remote_copy(
+            src_ref=source,
+            dst_ref=target,
+            send_sem=es.at[i],
+            recv_sem=er.at[i],
+            device_id={"sec": device},
+            device_id_type=MESH,
+        )
+
+    def helper_copies(device):
+        return to_helper(0, rbuf, rx, device), to_helper(1, rtagstage, rtag, device)
+
+    def result_copy(device):
+        return to_helper(2, fstage, fbuf, device)
+
+    if proxied:
+
+        @pl.when(is_end)
+        def _():
+            for k in range(per):
+                right = right_of_ref[far * per + k]
+                for b in range(rights):
+                    flag = jnp.where(right == b, 1.0, 0.0)
+                    rtagstage[k, b] = jnp.full((16, 128), flag, F32).astype(BF)
+            for copy in helper_copies(helper):
+                copy.start()
+
+    def spread(flag, columns):
+        flag = jnp.concatenate([flag] * (columns // 128), axis=1)
+        return jnp.concatenate([flag] * (width // 16), axis=0)
+
+    def compute_moved(q):
+        for k in range(per):
+            x = jnp.concatenate([wbuf[n, 0, k], wbuf[n, 1, k]], axis=1)
+            env = lbuf[far, q, 0] * spread(tagbuf[n, k, 0], width)
+            for l in range(1, lefts):
+                env = env + lbuf[far, q, l] * spread(tagbuf[n, k, l], width)
+            renv = rx[0, q] * spread(rtag[k, 0], half)
+            for b in range(1, rights):
+                renv = renv + rx[b, q] * spread(rtag[k, b], half)
+            y = jnp.dot(env, x, preferred_element_type=F32).astype(BF)
+            total[n, k] += jnp.dot(y, renv, preferred_element_type=F32)
+
+        @pl.when(q == nw - 1)
+        def _():
+            for k in range(per):
+                rounded[n, k] = total[n, k].astype(BF)
+            for o in range(1, mpos):
+                partial_to(n, o).start()
 
     def compute(d, q):
         for k in range(per):
@@ -282,7 +360,7 @@
             total[d, k] = jnp.zeros((width, half), F32)
         return carry
 
-    lax.fori_loop(0, n, clear, 0)
+    lax.fori_loop(0, n + 1 if proxied else n, clear, 0)
 
     wave_cross(me, other).wait_recv()
 
@@ -292,16 +370,25 @@
 
     lax.fori_loop(0, nw, first, 0)
 
+    def receive(d, slot):
+        tags(d, slot, d).wait_recv()
+        wave(d, slot, d).wait_recv()
+        for o in range(1, mpos):
+            wave_share(slot, o).start()
+        for o in range(1, mpos):
+            wave_shared(slot, o).wait_recv()
+        wave_cross(slot, c).start()
+
     def arrive(t, q):
         for step in (1, -1):
             d = me - step * t
 
-            @pl.when(jnp.logical_and(d >= 0, d < n))
+            @pl.when(both(d >= 0, d < n, jnp.logical_not(moved(d, me))))
             def _():
                 hop(d, q, -step, ls.at[d, q]).wait_recv()
                 nxt = me + step
 
-                @pl.when(jnp.logical_and(nxt >= 0, nxt < n))
+                @pl.when(both(nxt >= 0, nxt < n, jnp.logical_not(moved(d, nxt))))
                 def _():
                     hop(d, q, step, ls.at[d, q]).start()
 
@@ -309,19 +396,19 @@
 
                 @pl.when(q == 0)
                 def _():
-                    tags(d, d).wait_recv()
-                    wave(d, d).wait_recv()
-                    for o in range(1, mpos):
-                        wave_share(d, o).start()
-                    for o in range(1, mpos):
-                        wave_shared(d, o).wait_recv()
-                    wave_cross(d, c).start()
+                    receive(d, d)
+
+                if proxied:
+
+                    @pl.when(both(q == 0, is_proxy, d == far))
+                    def _():
+                        receive(d, n)
 
     def finish(t, q):
         for step in (1, -1):
             d = me - step * t
 
-            @pl.when(jnp.logical_and(d >= 0, d < n))
+            @pl.when(both(d >= 0, d < n, jnp.logical_not(moved(d, me))))
             def _():
                 @pl.when(q == 0)
                 def _():
@@ -330,6 +417,18 @@
                 cross(d, q).wait_recv()
                 compute(d, q)
 
+                if proxied:
+
+                    @pl.when(both(is_proxy, d == far))
+                    def _():
+                        @pl.when(q == 0)
+                        def _():
+                            wave_cross(n, other).wait_recv()
+                            for copy in helper_copies(end):
+                                copy.wait_recv()
+
+                        compute_moved(q)
+
     def turn(u, carry):
         @pl.when(u < (n - 1) * nw)
         def _():
@@ -343,6 +442,34 @@
 
     lax.fori_loop(0, (n - 1) * nw + 1, turn, 0)
 
+    if proxied:
+
+        @pl.when(is_proxy)
+        def _():
+            for o in range(1, mpos):
+                partial_to(n, o).wait_recv()
+            for k in range(per):
+                value = total[n, k, own, :]
+                for o in range(1, mpos):
+                    value = value + mbuf[o - 1, n, k].astype(F32)
+                fstage[k] = value.astype(BF)
+            result_copy(end).start()
+            wave_cross(n, c).wait_send()
+            for o in range(1, mpos):
+                partial_to(n, o).wait_send()
+                wave_share(n, o).wait_send()
+            result_copy(end).wait_send()
+
+        @pl.when(is_end)
+        def _():
+            for copy in helper_copies(helper):
+                copy.wait_send()
+            result_copy(helper).wait_recv()
+            for k in range(per):
+                total[far, k, own, :] = fbuf[k].astype(F32)
+                for o in range(1, mpos):
+                    mbuf[o - 1, far, k] = jnp.zeros((mrows, half), BF)
+
     for q in range(nw):
 
         @pl.when(me + 1 < n)
@@ -354,25 +481,30 @@
             hop(me, q, -1, ls_own.at[1, q]).wait_send()
 
     def drain(d, carry):
-        wave_cross(d, c).wait_send()
-        for o in range(1, mpos):
-            partial_to(d, o).wait()
+        @pl.when(jnp.logical_not(moved(d, me)))
+        def _():
+            wave_cross(d, c).wait_send()
+            for o in range(1, mpos):
+                partial_to(d, o).wait()
 
         @pl.when(d != me)
         def _():
-            wave(d, me).wait_send()
+            wave(d, me, d).wait_send()
+            tags(d, me, d).wait_send()
+
+        @pl.when(both(d != me, jnp.logical_not(moved(d, me))))
+        def _():
             for o in range(1, mpos):
                 wave_share(d, o).wait_send()
-            tags(d, me).wait_send()
             for q in range(nw):
                 cross(d, q).wait_send()
 
-        @pl.when(jnp.logical_and(d < me, me + 1 < n))
+        @pl.when(both(d < me, me + 1 < n, jnp.logical_not(moved(d, me + 1))))
         def _():
             for q in range(nw):
                 hop(d, q, 1, ls.at[d, q]).wait_send()
 
-        @pl.when(jnp.logical_and(d > me, me > 0))
+        @pl.when(both(d > me, me > 0, jnp.logical_not(moved(d, me - 1))))
         def _():
             for q in range(nw):
                 hop(d, q, -1, ls.at[d, q]).wait_send()
@@ -416,7 +548,7 @@
     return pl.pallas_call(
         functools.partial(kernel, n, mpos),
         out_shape=jax.ShapeDtypeStruct((pairs, width // mpos, half), BF),
-        in_specs=[pl.BlockSpec(memory_space=pl.ANY)] * 10,
+        in_specs=[pl.BlockSpec(memory_space=pltpu.HBM)] * 10,
         out_specs=vmem,
         scratch_shapes=[
             pltpu.VMEM(wavefunction.shape, BF),
@@ -436,26 +568,33 @@
             pltpu.VMEM(right_env.shape, BF),
             pltpu.VMEM((n, per, width, half), BF),
             pltpu.VMEM((n, per, lefts, 16, 128), BF),
-            pltpu.VMEM((n, 2, per, width, half), BF),
-            pltpu.VMEM((n, per, lefts, 16, 128), BF),
-            pltpu.VMEM((n, per, width, half), F32),
-            pltpu.VMEM((n, per, width, half), BF),
-            pltpu.VMEM((others, n, per, width // mpos, half), BF),
+            pltpu.VMEM((n + 1, 2, per, width, half), BF),
+            pltpu.VMEM((n + 1, per, lefts, 16, 128), BF),
+            pltpu.VMEM((n + 1, per, width, half), F32),
+            pltpu.VMEM((n + 1, per, width, half), BF),
+            pltpu.VMEM((others, n + 1, per, width // mpos, half), BF),
             dma((2, nw)),
             dma((n, nw)),
             dma((n, nw)),
             dma((n, nw)),
             dma((n, nw)),
-            dma((n,)),
-            dma((n,)),
-            dma((n, others)),
-            dma((n, others)),
-            dma((n,)),
-            dma((n,)),
-            dma((n,)),
-            dma((n,)),
-            dma((n, others)),
-            dma((n, others)),
+            dma((n + 1,)),
+            dma((n + 1,)),
+            dma((n + 1, others)),
+            dma((n + 1, others)),
+            dma((n + 1,)),
+            dma((n + 1,)),
+            dma((n + 1,)),
+            dma((n + 1,)),
+            dma((n + 1, others)),
+            dma((n + 1, others)),
+            pltpu.VMEM(right_env.shape, BF),
+            pltpu.VMEM((per, right_env.shape[0], 16, 128), BF),
+            pltpu.VMEM((per, right_env.shape[0], 16, 128), BF),
+            pltpu.VMEM((per, width // mpos, half), BF),
+            pltpu.VMEM((per, width // mpos, half), BF),
+            dma((3,)),
+            dma((3,)),
         ],
         compiler_params=pltpu.CompilerParams(
             collective_id=0, has_side_effects=True, vmem_limit_bytes=52 * 1024 * 1024

time: 80.5 us -> 83.3 us (1.035)
  Pallas kernels: 73.7 us -> 76.6 us
    pallas_call x1, Pallas kernels: 73.7 us -> 76.6 us  [local(): pl.pallas_call(functools.partial(kernel, n, mpos), out_shape=jax.ShapeDty...]
where the time goes in v5:
time: 83.3 us; the launch traced here: 83.1 us
  Pallas kernels  76.6 us (92%)
  local copies, waits for them, and re-layouts  6.49 us (8%)
    pallas_call x1, Pallas kernels, local(): pl.pallas_call(functools.partial(kernel, n, mpos), out_shape=jax.ShapeDty...  76.6 us
    unnamed x17, local copies, waits for them, and re-layouts  6.49 us

profile of v5, /device:TPU:0, one launch (start us, length us, event | category | flops | bytes accessed | tf_op | source)
XLA Modules:
  0.0 83.1 jit_solution(6744673778711391770)
XLA Ops:
  0.0 0.0 copy-start
  0.0 1.1 %copy-done = bf16[2,5,256,128]{3,2,1,0:T(8,128)(2,1)S(1)} copy-done((bf16[2,5,256,128]{3,2,1,0:T(8,128)(2,1)S(1)}, bf16[2,5,256,128]{3,2,1,0:T(8,128)(2,1)}, u32[]{:S(2)}) %copy-start) | copy-done | bytes 655384
  1.1 0.0 copy-start.1
  1.1 0.7 copy-done.1
  1.8 0.0 copy-start.2
  1.8 0.7 copy-done.2
  2.4 0.0 copy-start.3
  2.4 0.7 copy-done.3
  3.1 0.0 copy-start.4
  3.1 0.7 copy-done.4
  3.7 0.0 copy-start.5
  3.7 0.7 copy-done.5
  4.4 0.0 copy-start.6
  4.4 0.7 copy-done.6
  5.0 0.0 copy-start.7
  5.0 0.7 copy-done.7
  5.7 76.6 %apply_blocks.1 = bf16[16,128,128]{2,1,0:T(8,128)(2,1)S(1)} custom-call(s32[1,16]{1,0:T(1,128)S(1)} %copy-done.2, s32[1,16]{1,0:T(1,128)S(1)} %copy-done.3, s32[1,16]{1,0:T(1,128)S(1)} %copy-done.4, s32[1,16]{1,0:T(1,128)S(1)} %copy-done.5, s32[2]{0:T(128)S(1)} %copy-done.6, s32[2]{0:T(128)S(1)} %copy-done.7, s32[2,5]{1,0:T(2,128)S(1)} %copy-done.1, ...), custom_call_target="tpu_custom_call" | custom-call | flops 4026531840 | bytes 4194304 | tf_op jit(solution)/shard_map/apply_blocks/pallas_call | solution.py:548
  82.3 0.8 copy.12
Async XLA Ops:
  0.0 1.1 %copy-start = (bf16[2,5,256,128]{3,2,1,0:T(8,128)(2,1)S(1)}, bf16[2,5,256,128]{3,2,1,0:T(8,128)(2,1)}, u32[]{:S(2)}) copy-start(bf16[2,5,256,128]{3,2,1,0:T(8,128)(2,1)} %right_hbm.1) | copy-start | bytes 1966084
  1.1 0.7 copy-start.1
  1.8 0.7 copy-start.2
  2.4 0.7 copy-start.3
  3.1 0.7 copy-start.4
  3.7 0.7 copy-start.5
  4.4 0.7 copy-start.6
  5.0 0.7 copy-start.7

commit v6 on v4

--- a/solution.py
+++ b/solution.py
@@ -416,7 +416,7 @@
     return pl.pallas_call(
         functools.partial(kernel, n, mpos),
         out_shape=jax.ShapeDtypeStruct((pairs, width // mpos, half), BF),
-        in_specs=[pl.BlockSpec(memory_space=pl.ANY)] * 10,
+        in_specs=[pl.BlockSpec(memory_space=pltpu.HBM)] * 10,
         out_specs=vmem,
         scratch_shapes=[
             pltpu.VMEM(wavefunction.shape, BF),
@@ -458,7 +458,7 @@
             dma((n, others)),
         ],
         compiler_params=pltpu.CompilerParams(
-            collective_id=0, has_side_effects=True, vmem_limit_bytes=52 * 1024 * 1024
+            collective_id=0, has_side_effects=True, vmem_limit_bytes=64 * 1024 * 1024
         ),
         cost_estimate=pl.CostEstimate(
             flops=6 * pairs * nw * width * width * half,

time: 80.5 us -> 76.4 us (0.949)
  local copies, waits for them, and re-layouts: 6.49 us -> 1.89 us
    unnamed x17 -> x1, local copies, waits for them, and re-layouts: 6.49 us -> 1.89 us
where the time goes in v6:
time: 76.4 us; the launch traced here: 76.2 us
  Pallas kernels  74.3 us (97%)
  local copies, waits for them, and re-layouts  1.89 us (2%)
    pallas_call x1, Pallas kernels, local(): pl.pallas_call(functools.partial(kernel, n, mpos), out_shape=jax.ShapeDty...  74.3 us
    unnamed x1, local copies, waits for them, and re-layouts  1.89 us

profile of v6, /device:TPU:0, one launch (start us, length us, event | category | flops | bytes accessed | tf_op | source)
XLA Modules:
  0.0 76.2 jit_solution(11759104313255321156)
XLA Ops:
  0.0 74.3 %apply_blocks.1 = bf16[16,128,128]{2,1,0:T(8,128)(2,1)} custom-call(s32[1,16]{1,0:T(1,128)} %send_hbm.1, s32[1,16]{1,0:T(1,128)} %recv_hbm.1, s32[1,16]{1,0:T(1,128)} %pair_hbm.1, s32[1,16]{1,0:T(1,128)} %pair_right_hbm.1, s32[2]{0:T(128)} %lsize_hbm.1, s32[2]{0:T(128)} %rsize_hbm.1, s32[2,5]{1,0:T(2,128)} %pattern_hbm.1, bf16[16,256,128]{2,1,0:T(8,128)(2,1)} %wf_hbm.1, ...), custom_call_target="tpu_custom_call" | custom-call | flops 4026531840 | bytes 4194304 | tf_op jit(solution)/shard_map/apply_blocks/pallas_call | solution.py:416
  74.3 1.9 %copy.12 = bf16[16,128,128]{2,1,0:T(8,128)(2,1)} copy(bf16[16,128,128]{2,1,0:T(8,128)(2,1)} %apply_blocks.1) | data formatting | bytes 1048576

commit v7 on v6

--- a/solution.py
+++ b/solution.py
@@ -200,22 +200,7 @@
     for copy in small:
         copy.wait()
     keeps = [jnp.where(row < lsize_ref[l], 1.0, 0.0) for l in range(lefts)]
-    load_left.wait()
-    for q in range(nw):
-        for l in range(lefts):
-            scale = (keeps[l] * pattern_ref[l, q].astype(F32)).astype(BF)
-            lbuf[me, q, l] = left_ref[l, q] * scale
-        if q == 0:
-            pl.semaphore_wait(barrier, n + mpos - 1)
-
-        @pl.when(me + 1 < n)
-        def _():
-            hop(me, q, 1, ls_own.at[0, q]).start()
-
-        @pl.when(me > 0)
-        def _():
-            hop(me, q, -1, ls_own.at[1, q]).start()
-
+    pl.semaphore_wait(barrier, n + mpos - 1)
     load_wf.wait()
 
     def fill(e, carry):
@@ -236,6 +221,21 @@
         return carry
 
     lax.fori_loop(0, n, fill, 0)
+
+    load_left.wait()
+    for q in range(nw):
+        for l in range(lefts):
+            scale = (keeps[l] * pattern_ref[l, q].astype(F32)).astype(BF)
+            lbuf[me, q, l] = left_ref[l, q] * scale
+
+        @pl.when(me + 1 < n)
+        def _():
+            hop(me, q, 1, ls_own.at[0, q]).start()
+
+        @pl.when(me > 0)
+        def _():
+            hop(me, q, -1, ls_own.at[1, q]).start()
+
     wbuf[me, c] = stage[me]
     tagbuf[me] = tagstage[me]
     wave_cross(me, c).start()

time: 76.4 us -> 70.4 us (0.921)
  Pallas kernels: 74.3 us -> 68.4 us
    pallas_call x1, Pallas kernels: 74.3 us -> 68.4 us  [local(): pl.pallas_call(functools.partial(kernel, n, mpos), out_shape=jax.ShapeDty...]
where the time goes in v7:
time: 70.4 us; the launch traced here: 70.3 us
  Pallas kernels  68.4 us (97%)
  local copies, waits for them, and re-layouts  1.89 us (3%)
    pallas_call x1, Pallas kernels, local(): pl.pallas_call(functools.partial(kernel, n, mpos), out_shape=jax.ShapeDty...  68.4 us
    unnamed x1, local copies, waits for them, and re-layouts  1.89 us

profile of v7, /device:TPU:0, one launch (start us, length us, event | category | flops | bytes accessed | tf_op | source)
XLA Modules:
  0.0 70.3 jit_solution(17300811590860370254)
XLA Ops:
  0.0 68.4 %apply_blocks.1 = bf16[16,128,128]{2,1,0:T(8,128)(2,1)} custom-call(s32[1,16]{1,0:T(1,128)} %send_hbm.1, s32[1,16]{1,0:T(1,128)} %recv_hbm.1, s32[1,16]{1,0:T(1,128)} %pair_hbm.1, s32[1,16]{1,0:T(1,128)} %pair_right_hbm.1, s32[2]{0:T(128)} %lsize_hbm.1, s32[2]{0:T(128)} %rsize_hbm.1, s32[2,5]{1,0:T(2,128)} %pattern_hbm.1, bf16[16,256,128]{2,1,0:T(8,128)(2,1)} %wf_hbm.1, ...), custom_call_target="tpu_custom_call" | custom-call | flops 4026531840 | bytes 4194304 | tf_op jit(solution)/shard_map/apply_blocks/pallas_call | solution.py:416
  68.4 1.9 %copy.12 = bf16[16,128,128]{2,1,0:T(8,128)(2,1)} copy(bf16[16,128,128]{2,1,0:T(8,128)(2,1)} %apply_blocks.1) | data formatting | bytes 1048576
